TPU v7x, 32 devices: a whole 2x2x4 slice. The times are simulated.
32 devices in a mesh: groups: 2 (over x), rows: 16 (over z, y, core).
Axes of the slice: x: 2, y: 2, z: 4, core: 2. Of those that a mesh axis runs over, the one named last changes fastest.
Arguments:
- occupied: bfloat16 [8192, 512], P(('groups', 'rows')), parts along dimension 0, may hold values from -6 to 6
- occupied_scale: float32 [1024], P('groups'), parts along dimension 0, may hold values from 0.013258252 to 0.13258252
- virtual: bfloat16 [8192, 512], P(('groups', 'rows')), parts along dimension 0, may hold values from -6 to 6
- virtual_scale: float32 [1024], P('groups'), parts along dimension 0, may hold values from 0.013258252 to 0.13258252
- trial: bfloat16 [8192, 512], P(('groups', 'rows')), parts along dimension 0, may hold values from -0.09375 to 0.09375
Outputs:
- applied: float32 [8192, 512], P(('groups', 'rows')), parts along dimension 0
There are 2 independent parts, one for each index of `groups`. A program takes and returns all parts, laid end to end along the dimension named above; each array names one. Nothing has to cross between parts.
All inputs are finite; a program needn't handle non-finite values.
Results may differ from a plain program's by a relative error of at most 0.003.
Values may be sent and summed in bfloat16 or wider, within the bound.
A program may use at most 128 MiB of HBM per device.

v0:
```python
import jax
import jax.numpy as jnp
from jax import lax
from jax.sharding import PartitionSpec as P


def contract_rows(left, right):
    return lax.dot_general(
        left, right, (((1,), (1,)), ((), ())), preferred_element_type=jnp.float32
    )


def local(occupied, occupied_scale, virtual, virtual_scale, trial):
    scaled_occupied = (occupied.astype(jnp.float32) * occupied_scale[None, :]).astype(jnp.bfloat16)
    scaled_virtual = (virtual.astype(jnp.float32) * virtual_scale[None, :]).astype(jnp.bfloat16)
    remote_occupied = lax.all_gather(occupied, "rows", axis=0, tiled=True)
    remote_virtual = lax.all_gather(virtual, "rows", axis=0, tiled=True)
    remote_trial = lax.all_gather(trial, "rows", axis=0, tiled=True)
    green_occ = contract_rows(scaled_occupied, remote_occupied)
    green_vir = contract_rows(scaled_virtual, remote_virtual)
    response = (green_occ * green_vir).astype(jnp.bfloat16)
    return jnp.dot(response, remote_trial, preferred_element_type=jnp.float32)


def solution(mesh):
    in_specs = (
        P(("groups", "rows"), None),
        P("groups"),
        P(("groups", "rows"), None),
        P("groups"),
        P(("groups", "rows"), None),
    )
    out_specs = P(("groups", "rows"), None)
    return jax.shard_map(local, mesh=mesh, in_specs=in_specs, out_specs=out_specs, check_vma=False)
```

profile of v0, /device:TPU:0, one launch (start us, length us, event | category | flops | bytes accessed | tf_op | source)
XLA Modules:
  0.0 179.7 jit_solution(8943579784572050514)
XLA Ops:
  6.5 0.0 all-gather.4.cloned.1.call-start
  6.5 0.7 all-gather.4.cloned.1.call-update
  7.3 0.0 all-gather.8.cloned.1.call-start
  7.3 0.7 all-gather.8.cloned.1.call-update
  8.0 0.0 all-gather.6.cloned.1.call-start
  8.1 0.7 all-gather.6.cloned.1.call-update
  8.7 0.0 copy-start
  8.8 0.0 copy-start.1
  8.8 54.1 %all-gather.4.cloned.1.call-done = bf16[4096,512]{1,0:T(8,128)(2,1)} async-done(((bf16[256,512]{1,0:T(8,128)(2,1)}), bf16[4096,512]{1,0:T(8,128)(2,1)}) %all-gather.4.cloned.1.call-update) | async-done | bytes 4194320 | tf_op jit(solution)/shard_map/all_gather | solution.py:16
  62.8 5.5 %fusion.2 = f32[256,4096]{1,0:T(8,128)} fusion(bf16[4096,512]{1,0:T(8,128)(2,1)} %all-gather.4.cloned.1.call-done, bf16[256,512]{1,0:T(8,128)(2,1)} %param.5, f32[512]{0:T(512)} %param.6), kind=kOutput, calls=%fused_computation.5 | convolution fusion | flops 1074135040 | bytes 8652800 | tf_op jit(solution)/shard_map/dot_general | solution.py:8
  68.3 45.7 %all-gather.8.cloned.1.call-done = bf16[4096,512]{1,0:T(8,128)(2,1)} async-done(((bf16[256,512]{1,0:T(8,128)(2,1)}), bf16[4096,512]{1,0:T(8,128)(2,1)}) %all-gather.8.cloned.1.call-update) | async-done | bytes 4194320 | tf_op jit(solution)/shard_map/all_gather | solution.py:18
  114.1 51.3 %all-gather.6.cloned.1.call-done = bf16[4096,512]{1,0:T(8,128)(2,1)} async-done(((bf16[256,512]{1,0:T(8,128)(2,1)}), bf16[4096,512]{1,0:T(8,128)(2,1)}) %all-gather.6.cloned.1.call-update) | async-done | bytes 4194320 | tf_op jit(solution)/shard_map/all_gather | solution.py:17
  165.3 0.0 copy-done
  165.3 0.0 copy-done.1
  165.3 7.8 %fusion.1 = f32[256,512]{1,0:T(8,128)} fusion(bf16[4096,512]{1,0:T(8,128)(2,1)} %all-gather.8.cloned.1.call-done, f32[256,4096]{1,0:T(8,128)} %fusion.2, bf16[4096,512]{1,0:T(8,128)(2,1)} %all-gather.6.cloned.1.call-done, bf16[256,512]{1,0:T(8,128)(2,1)S(1)} %copy-done, f32[512]{0:T(512)S(1)} %copy-done.1), kind=kOutput, calls=%fused_computation.2 | convolution fusion | flops 2149974016 | bytes 13371392 | tf_op jit(solution)/shard_map/dot_general | solution.py:22
Async XLA Ops:
  6.5 56.3 %all-gather.4.cloned.1.call-start = ((), (), s32[]{:S(2)}) async-start(), calls=%async_computation | async-start | bytes 4456448 | tf_op jit(solution)/shard_map/all_gather | solution.py:16
  7.3 106.8 %all-gather.8.cloned.1.call-start = ((), (), s32[]{:S(2)}) async-start(), calls=%async_computation.2 | async-start | bytes 4456448 | tf_op jit(solution)/shard_map/all_gather | solution.py:18
  8.0 157.3 %all-gather.6.cloned.1.call-start = ((), (), s32[]{:S(2)}) async-start(), calls=%async_computation.1 | async-start | bytes 4456448 | tf_op jit(solution)/shard_map/all_gather | solution.py:17
  8.7 156.6 %copy-start = (bf16[256,512]{1,0:T(8,128)(2,1)S(1)}, bf16[256,512]{1,0:T(8,128)(2,1)}, u32[]{:S(2)}) copy-start(bf16[256,512]{1,0:T(8,128)(2,1)} %param.7) | copy-start | bytes 786436
  8.8 156.6 %copy-start.1 = (f32[512]{0:T(512)S(1)}, f32[512]{0:T(512)}, u32[]{:S(2)}) copy-start(f32[512]{0:T(512)} %param.8) | copy-start | bytes 6148
Sparse Core Ops, SparseCore 0:
  9.5 53.2 all-gather.3
  65.0 49.0 all-gather.7
  116.2 49.0 all-gather.5
where the time goes:
time: 180 us
  waiting for transfers between devices  153 us (85%)
  matrix products  13.3 us (7%)
  between operations  13.1 us (7%)
    all_gather x1, waiting for transfers between devices, local(): remote_occupied = lax.all_gather(occupied, 'rows', axis=0, tiled=True)  54.1 us
    all_gather x1, waiting for transfers between devices, local(): remote_virtual = lax.all_gather(virtual, 'rows', axis=0, tiled=True)  51.3 us
    all_gather x1, waiting for transfers between devices, local(): remote_trial = lax.all_gather(trial, 'rows', axis=0, tiled=True)  45.7 us
    dot_general x1, matrix products, local(): return jnp.dot(response, remote_trial, preferred_element_type=jnp.float32)  7.83 us
    dot_general x1, matrix products, contract_rows(): lax.dot_general(left, right, (((1,), (1,)), ((), ())), preferred_element_...  5.52 us
  transfers between devices with their start and end apart: 3, of which 3 were waited for; matrix products, arithmetic and copies ran while one was open for 3% of the time, Pallas kernels for 0%

commit v1 on v0

v1 whole, which is shorter than its diff:
```python
import functools

import jax
import jax.numpy as jnp
from jax import lax
from jax.experimental import pallas as pl
from jax.experimental.pallas import tpu as pltpu
from jax.sharding import PartitionSpec as P

MESH = pl.DeviceIdType.MESH
NT = (((1,), (1,)), ((), ()))


def chip_columns(mesh):
    spots = {tuple(getattr(d, "coords", (0, 0, 0))[:2]) for d in mesh.devices[0].flat}
    return len(spots)


def kernel(chips, columns, occ_ref, os_ref, vir_ref, vs_ref, tri_ref, out_ref,
           buf, so, sv, ring_send, ring_recv, pair_send, pair_recv):
    group = lax.axis_index("groups")
    me = lax.axis_index("rows")
    core = lax.rem(me, 2)
    chip = me // 2
    half = buf.shape[-2]
    depth = chips // columns

    def place_of(q):
        if columns != 2:
            return q
        z, y = q // 2, lax.rem(q, 2)
        return z * (1 - y) + (2 * depth - 1 - z) * y

    def chip_at(p):
        if columns != 2:
            return p
        y = p // depth
        z = p * (1 - y) + (2 * depth - 1 - p) * y
        return z * 2 + y

    place = place_of(chip)
    after = chip_at(lax.rem(place + 1, chips)) * 2 + core
    before = chip_at(lax.rem(place + chips - 1, chips)) * 2 + core
    twin = chip * 2 + 1 - core

    barrier = pltpu.get_barrier_semaphore()
    for other in (after, before, twin):
        pl.semaphore_signal(barrier, inc=1, device_id=(group, other), device_id_type=MESH)

    own = []
    for a, ref in enumerate((occ_ref, vir_ref, tri_ref)):
        for d in range(2):
            copy = pltpu.make_async_copy(
                ref.at[pl.ds(d * half, half)], buf.at[a, d, place, core], ring_recv.at[a, d, 0])
            copy.start()
            own.append(copy)
    pl.semaphore_wait(barrier, 3)

    def slot_of(d, s):
        return lax.rem(place + (chips - s if d == 0 else s), chips)

    def ring_copy(a, d, s):
        block = buf.at[a, d, slot_of(d, s), core]
        return pltpu.make_async_remote_copy(
            src_ref=block, dst_ref=block, send_sem=ring_send.at[a, d, s],
            recv_sem=ring_recv.at[a, d, s + 1],
            device_id=(group, after if d == 0 else before), device_id_type=MESH)

    def pair_copy(a, d, s):
        block = buf.at[a, d, slot_of(d, s), core]
        return pltpu.make_async_remote_copy(
            src_ref=block, dst_ref=block, send_sem=pair_send.at[a, d, s],
            recv_sem=pair_recv.at[a, d, s],
            device_id=(group, twin), device_id_type=MESH)

    def arrived(a, d, s):
        block = buf.at[a, d, slot_of(d, s), core]
        pltpu.make_async_copy(block, block, ring_recv.at[a, d, s]).wait()

    def twin_arrived(a, d, s):
        block = buf.at[a, d, slot_of(d, s), 1 - core]
        pltpu.make_async_copy(block, block, pair_recv.at[a, d, s]).wait()

    def step(s, carry):
        for a in range(3):
            for d in range(2):
                arrived(a, d, s)

                @pl.when(s < chips - 1)
                def _():
                    ring_copy(a, d, s).start()

                pair_copy(a, d, s).start()

        @pl.when(s == 0)
        def _():
            so[...] = (occ_rows(0) * os_ref[...]).astype(jnp.bfloat16)
            sv[...] = (occ_rows(1) * vs_ref[...]).astype(jnp.bfloat16)
            out_ref[...] = jnp.zeros_like(out_ref)

        for d in range(2):
            for a in range(3):
                twin_arrived(a, d, s)
            slot = slot_of(d, s)
            rows = [buf[a, d, slot].reshape(2 * half, buf.shape[-1]) for a in range(3)]
            green_occ = lax.dot_general(so[...], rows[0], NT, preferred_element_type=jnp.float32)
            green_vir = lax.dot_general(sv[...], rows[1], NT, preferred_element_type=jnp.float32)
            response = (green_occ * green_vir).astype(jnp.bfloat16)
            out_ref[...] += jnp.dot(response, rows[2], preferred_element_type=jnp.float32)
        return carry

    def occ_rows(a):
        return jnp.concatenate([buf[a, d, place, core] for d in range(2)], axis=0).astype(jnp.float32)

    lax.fori_loop(0, chips, step, 0)

    def finish(s, carry):
        for a in range(3):
            for d in range(2):
                @pl.when(s < chips - 1)
                def _():
                    ring_copy(a, d, s).wait_send()

                pair_copy(a, d, s).wait_send()
        return carry

    lax.fori_loop(0, chips, finish, 0)


def local(chips, columns, occupied, occupied_scale, virtual, virtual_scale, trial):
    rows, width = occupied.shape
    any_space = pl.BlockSpec(memory_space=pl.ANY)
    vmem = pl.BlockSpec(memory_space=pltpu.VMEM)
    points = rows * 2 * chips
    sems = pltpu.SemaphoreType.DMA((3, 2, chips))
    return pl.pallas_call(
        functools.partial(kernel, chips, columns),
        out_shape=jax.ShapeDtypeStruct((rows, trial.shape[1]), jnp.float32),
        in_specs=[any_space, vmem, any_space, vmem, any_space],
        out_specs=vmem,
        scratch_shapes=[
            pltpu.VMEM((3, 2, chips, 2, rows // 2, width), jnp.bfloat16),
            pltpu.VMEM((rows, width), jnp.bfloat16),
            pltpu.VMEM((rows, width), jnp.bfloat16),
            sems, sems, sems, sems,
        ],
        compiler_params=pltpu.CompilerParams(
            collective_id=0, has_side_effects=True, vmem_limit_bytes=48 * 1024 * 1024),
        cost_estimate=pl.CostEstimate(
            flops=6 * rows * points * width, bytes_accessed=8 * rows * width, transcendentals=0),
    )(occupied, occupied_scale[None, :], virtual, virtual_scale[None, :], trial)


def solution(mesh):
    spread, scale = P(("groups", "rows"), None), P("groups")
    body = functools.partial(local, mesh.shape["rows"] // 2, chip_columns(mesh))
    return jax.shard_map(
        body, mesh=mesh, in_specs=(spread, scale, spread, scale, spread),
        out_specs=spread, check_vma=False)
```

time: 180 us -> 72.8 us (0.40)
  waiting for transfers between devices: 153 us -> 0 us
  Pallas kernels: 0 us -> 66.8 us
  matrix products: 13.3 us -> 0 us
  between operations: 13.1 us -> 0.01 us
  local copies, waits for them, and re-layouts: 0.01 us -> 5.01 us
    all_gather x3 -> x0, waiting for transfers between devices: 151 us -> none  [the longest x1 54.1 us: local(): remote_occupied = lax.all_gather(occupied, 'rows', axis=0, tiled=True)]
    pallas_call x0 -> x1, Pallas kernels: none -> 66.8 us  [local(): pl.pallas_call(functools.partial(kernel, chips, columns), out_shape=jax.S...]
    dot_general x2 -> x0, matrix products: 13.3 us -> none  [the longest x1 7.83 us: local(): return jnp.dot(response, remote_trial, preferred_element_type=jnp.float32)]
    unnamed x4 -> x11, local copies, waits for them, and re-layouts: 0.01 us -> 5.01 us
    unnamed x3 -> x0, waiting for transfers between devices: 2.09 us -> none
  transfers between devices with their start and end apart: 3 -> 0, of which waited for: 3 -> 0; matrix products, arithmetic and copies ran while one was open for 3% -> 0% of each run, Pallas kernels for 0% -> 0%
where the time goes in v1:
time: 72.8 us; the launch traced here: 71.8 us
  Pallas kernels  66.8 us (92%)
  local copies, waits for them, and re-layouts  5.01 us (7%)
    pallas_call x1, Pallas kernels, local(): pl.pallas_call(functools.partial(kernel, chips, columns), out_shape=jax.S...  66.8 us
    unnamed x11, local copies, waits for them, and re-layouts  5.01 us

profile of v1, /device:TPU:0, one launch (start us, length us, event | category | flops | bytes accessed | tf_op | source)
XLA Modules:
  0.0 71.8 jit_solution(17055209878273065726)
XLA Ops:
  0.0 0.0 copy-start.3
  0.0 0.7 copy-done.3
  0.7 0.0 copy-start
  0.7 0.9 %copy-done = bf16[256,512]{1,0:T(8,128)(2,1)S(1)} copy-done((bf16[256,512]{1,0:T(8,128)(2,1)S(1)}, bf16[256,512]{1,0:T(8,128)(2,1)}, u32[]{:S(2)}) %copy-start) | copy-done | bytes 262168
  1.6 0.0 copy-start.1
  1.6 0.9 %copy-done.1 = bf16[256,512]{1,0:T(8,128)(2,1)S(1)} copy-done((bf16[256,512]{1,0:T(8,128)(2,1)S(1)}, bf16[256,512]{1,0:T(8,128)(2,1)}, u32[]{:S(2)}) %copy-start.1) | copy-done | bytes 262168
  2.6 0.0 copy-start.2
  2.6 0.9 %copy-done.2 = bf16[256,512]{1,0:T(8,128)(2,1)S(1)} copy-done((bf16[256,512]{1,0:T(8,128)(2,1)S(1)}, bf16[256,512]{1,0:T(8,128)(2,1)}, u32[]{:S(2)}) %copy-start.2) | copy-done | bytes 262168
  3.5 0.0 copy-start.4
  3.5 0.7 copy-done.4
  4.2 66.8 %shard_map.55 = f32[256,512]{1,0:T(8,128)S(1)} custom-call(bf16[256,512]{1,0:T(8,128)(2,1)S(1)} %copy-done, f32[1,512]{1,0:T(1,128)S(1)} %bitcast.2, bf16[256,512]{1,0:T(8,128)(2,1)S(1)} %copy-done.1, f32[1,512]{1,0:T(1,128)S(1)} %bitcast.3, bf16[256,512]{1,0:T(8,128)(2,1)S(1)} %copy-done.2), custom_call_target="tpu_custom_call" | custom-call | flops 3221225472 | bytes 1048576 | tf_op jit(solution)/shard_map/pallas_call | solution.py:136
  71.0 0.8 %copy.7 = f32[256,512]{1,0:T(8,128)} copy(f32[256,512]{1,0:T(8,128)S(1)} %shard_map.55) | data formatting | bytes 1048576
Async XLA Ops:
  0.0 0.7 copy-start.3
  0.7 0.9 %copy-start = (bf16[256,512]{1,0:T(8,128)(2,1)S(1)}, bf16[256,512]{1,0:T(8,128)(2,1)}, u32[]{:S(2)}) copy-start(bf16[256,512]{1,0:T(8,128)(2,1)} %occ_ref.1) | copy-start | bytes 786436
  1.6 0.9 %copy-start.1 = (bf16[256,512]{1,0:T(8,128)(2,1)S(1)}, bf16[256,512]{1,0:T(8,128)(2,1)}, u32[]{:S(2)}) copy-start(bf16[256,512]{1,0:T(8,128)(2,1)} %vir_ref.1) | copy-start | bytes 786436
  2.6 0.9 %copy-start.2 = (bf16[256,512]{1,0:T(8,128)(2,1)S(1)}, bf16[256,512]{1,0:T(8,128)(2,1)}, u32[]{:S(2)}) copy-start(bf16[256,512]{1,0:T(8,128)(2,1)} %tri_ref.1) | copy-start | bytes 786436
  3.5 0.7 copy-start.4

commit v2 on v1

--- a/solution.py
+++ b/solution.py
@@ -17,7 +17,7 @@
 
 
 def kernel(chips, columns, occ_ref, os_ref, vir_ref, vs_ref, tri_ref, out_ref,
-           buf, so, sv, ring_send, ring_recv, pair_send, pair_recv):
+           buf, scales, so, sv, ring_send, ring_recv, pair_send, pair_recv, scale_sem):
     group = lax.axis_index("groups")
     me = lax.axis_index("rows")
     core = lax.rem(me, 2)
@@ -47,13 +47,14 @@
     for other in (after, before, twin):
         pl.semaphore_signal(barrier, inc=1, device_id=(group, other), device_id_type=MESH)
 
-    own = []
     for a, ref in enumerate((occ_ref, vir_ref, tri_ref)):
         for d in range(2):
             copy = pltpu.make_async_copy(
                 ref.at[pl.ds(d * half, half)], buf.at[a, d, place, core], ring_recv.at[a, d, 0])
             copy.start()
-            own.append(copy)
+    loads = [pltpu.make_async_copy(ref, scales.at[a], scale_sem.at[a]) for a, ref in enumerate((os_ref, vs_ref))]
+    for copy in loads:
+        copy.start()
     pl.semaphore_wait(barrier, 3)
 
     def slot_of(d, s):
@@ -94,8 +95,10 @@
 
         @pl.when(s == 0)
         def _():
-            so[...] = (occ_rows(0) * os_ref[...]).astype(jnp.bfloat16)
-            sv[...] = (occ_rows(1) * vs_ref[...]).astype(jnp.bfloat16)
+            for copy in loads:
+                copy.wait()
+            so[...] = (occ_rows(0) * scales[0]).astype(jnp.bfloat16)
+            sv[...] = (occ_rows(1) * scales[1]).astype(jnp.bfloat16)
             out_ref[...] = jnp.zeros_like(out_ref)
 
         for d in range(2):
@@ -136,16 +139,17 @@
     return pl.pallas_call(
         functools.partial(kernel, chips, columns),
         out_shape=jax.ShapeDtypeStruct((rows, trial.shape[1]), jnp.float32),
-        in_specs=[any_space, vmem, any_space, vmem, any_space],
+        in_specs=[any_space] * 5,
         out_specs=vmem,
         scratch_shapes=[
             pltpu.VMEM((3, 2, chips, 2, rows // 2, width), jnp.bfloat16),
+            pltpu.VMEM((2, 1, width), jnp.float32),
             pltpu.VMEM((rows, width), jnp.bfloat16),
             pltpu.VMEM((rows, width), jnp.bfloat16),
-            sems, sems, sems, sems,
+            sems, sems, sems, sems, pltpu.SemaphoreType.DMA((2,)),
         ],
         compiler_params=pltpu.CompilerParams(
-            collective_id=0, has_side_effects=True, vmem_limit_bytes=48 * 1024 * 1024),
+            collective_id=0, has_side_effects=True, vmem_limit_bytes=60 * 1024 * 1024),
         cost_estimate=pl.CostEstimate(
             flops=6 * rows * points * width, bytes_accessed=8 * rows * width, transcendentals=0),
     )(occupied, occupied_scale[None, :], virtual, virtual_scale[None, :], trial)

time: 72.8 us -> 70.4 us (0.967)
  local copies, waits for them, and re-layouts: 5.01 us -> 1.87 us
  Pallas kernels: 66.8 us -> 67.6 us
    unnamed x11 -> x1, local copies, waits for them, and re-layouts: 5.01 us -> 1.87 us
    pallas_call x1, Pallas kernels: 66.8 us -> 67.6 us  [local(): pl.pallas_call(functools.partial(kernel, chips, columns), out_shape=jax.S...]
where the time goes in v2:
time: 70.4 us; the launch traced here: 69.5 us
  Pallas kernels  67.6 us (96%)
  local copies, waits for them, and re-layouts  1.87 us (3%)
    pallas_call x1, Pallas kernels, local(): pl.pallas_call(functools.partial(kernel, chips, columns), out_shape=jax.S...  67.6 us
    unnamed x1, local copies, waits for them, and re-layouts  1.87 us

profile of v2, /device:TPU:0, one launch (start us, length us, event | category | flops | bytes accessed | tf_op | source)
XLA Modules:
  0.0 69.5 jit_solution(5403530618496627226)
XLA Ops:
  0.0 67.6 %shard_map.55 = f32[256,512]{1,0:T(8,128)} custom-call(bf16[256,512]{1,0:T(8,128)(2,1)} %occ_ref.1, f32[1,512]{1,0:T(1,128)} %bitcast.2, bf16[256,512]{1,0:T(8,128)(2,1)} %vir_ref.1, f32[1,512]{1,0:T(1,128)} %bitcast.3, bf16[256,512]{1,0:T(8,128)(2,1)} %tri_ref.1), custom_call_target="tpu_custom_call" | custom-call | flops 3221225472 | bytes 1048576 | tf_op jit(solution)/shard_map/pallas_call | solution.py:139
  67.6 1.9 %copy.7 = f32[256,512]{1,0:T(8,128)} copy(f32[256,512]{1,0:T(8,128)} %shard_map.55) | data formatting | bytes 1048576

commit v3 on v2

--- a/solution.py
+++ b/solution.py
@@ -17,12 +17,14 @@
 
 
 def kernel(chips, columns, occ_ref, os_ref, vir_ref, vs_ref, tri_ref, out_ref,
-           buf, scales, so, sv, ring_send, ring_recv, pair_send, pair_recv, scale_sem):
+           buf, scales, so, sv, guest, part, back, came,
+           ring_send, ring_recv, pair_send, pair_recv, back_send, back_recv, scale_sem):
     group = lax.axis_index("groups")
     me = lax.axis_index("rows")
     core = lax.rem(me, 2)
     chip = me // 2
     half = buf.shape[-2]
+    reach = chips // 2
     depth = chips // columns
 
     def place_of(q):
@@ -82,52 +84,103 @@
         block = buf.at[a, d, slot_of(d, s), 1 - core]
         pltpu.make_async_copy(block, block, pair_recv.at[a, d, s]).wait()
 
+    def scaled(a, rows):
+        return (rows.astype(jnp.float32) * scales[a]).astype(jnp.bfloat16)
+
+    def product(left_occ, left_vir, d, slot):
+        rows = [buf[a, d, slot].reshape(2 * half, buf.shape[-1]) for a in range(3)]
+        green_occ = lax.dot_general(left_occ, rows[0], NT, preferred_element_type=jnp.float32)
+        green_vir = lax.dot_general(left_vir, rows[1], NT, preferred_element_type=jnp.float32)
+        response = (green_occ * green_vir).astype(jnp.bfloat16)
+        return jnp.dot(response, rows[2], preferred_element_type=jnp.float32)
+
+    def receive(s, forward):
+        for a in range(3):
+            for d in range(2):
+                arrived(a, d, s)
+                if forward:
+                    ring_copy(a, d, s).start()
+                pair_copy(a, d, s).start()
+
+    def receive_twin(s):
+        for d in range(2):
+            for a in range(3):
+                twin_arrived(a, d, s)
+
     def step(s, carry):
-        for a in range(3):
-            for d in range(2):
-                arrived(a, d, s)
-
-                @pl.when(s < chips - 1)
-                def _():
-                    ring_copy(a, d, s).start()
-
-                pair_copy(a, d, s).start()
+        receive(s, True)
 
         @pl.when(s == 0)
         def _():
             for copy in loads:
                 copy.wait()
-            so[...] = (occ_rows(0) * scales[0]).astype(jnp.bfloat16)
-            sv[...] = (occ_rows(1) * scales[1]).astype(jnp.bfloat16)
+            for d in range(2):
+                so[pl.ds(d * half, half)] = scaled(0, buf[0, d, place, core])
+                sv[pl.ds(d * half, half)] = scaled(1, buf[1, d, place, core])
             out_ref[...] = jnp.zeros_like(out_ref)
 
-        for d in range(2):
-            for a in range(3):
-                twin_arrived(a, d, s)
-            slot = slot_of(d, s)
-            rows = [buf[a, d, slot].reshape(2 * half, buf.shape[-1]) for a in range(3)]
-            green_occ = lax.dot_general(so[...], rows[0], NT, preferred_element_type=jnp.float32)
-            green_vir = lax.dot_general(sv[...], rows[1], NT, preferred_element_type=jnp.float32)
-            response = (green_occ * green_vir).astype(jnp.bfloat16)
-            out_ref[...] += jnp.dot(response, rows[2], preferred_element_type=jnp.float32)
+        @pl.when(s > 0)
+        def _():
+            for d in range(2):
+                slot = slot_of(d, s)
+                guest[d, s - 1, 0] = scaled(0, buf[0, d, slot, core])
+                guest[d, s - 1, 1] = scaled(1, buf[1, d, slot, core])
+                part[d, s - 1] = product(guest[d, s - 1, 0], guest[d, s - 1, 1], d, place)
+
+        receive_twin(s)
+        for d in range(2):
+            out_ref[...] += product(so[...], sv[...], d, slot_of(d, s))
         return carry
 
-    def occ_rows(a):
-        return jnp.concatenate([buf[a, d, place, core] for d in range(2)], axis=0).astype(jnp.float32)
-
-    lax.fori_loop(0, chips, step, 0)
+    lax.fori_loop(0, reach, step, 0)
+    receive(reach, False)
+    receive_twin(reach)
+
+    def back_copy(d, t):
+        return pltpu.make_async_remote_copy(
+            src_ref=back.at[d, t], dst_ref=came.at[d, t], send_sem=back_send.at[d, t],
+            recv_sem=back_recv.at[d, t],
+            device_id=(group, before if d == 0 else after), device_id_type=MESH)
+
+    def stage(t, first):
+        e = reach - 1 - t
+        for d in range(2):
+            total = part[d, e - 1] + product(
+                guest[d, e - 1, 0], guest[d, e - 1, 1], 1 - d, slot_of(1 - d, reach))
+            if not first:
+                back_copy(d, t - 1).wait_recv()
+                total += came[d, t - 1].astype(jnp.float32)
+            back[d, t] = total.astype(jnp.bfloat16)
+            back_copy(d, t).start()
+
+    stage(0, True)
+    for d in range(2):
+        out_ref[...] += product(so[...], sv[...], d, slot_of(d, reach))
+
+    def later_stage(t, carry):
+        stage(t, False)
+        return carry
+
+    lax.fori_loop(1, reach - 1, later_stage, 0)
+    for d in range(2):
+        back_copy(d, reach - 2).wait_recv()
+        out_ref[pl.ds(d * half, half)] += came[d, reach - 2].astype(jnp.float32)
 
     def finish(s, carry):
         for a in range(3):
             for d in range(2):
-                @pl.when(s < chips - 1)
+                @pl.when(s < reach)
                 def _():
                     ring_copy(a, d, s).wait_send()
 
                 pair_copy(a, d, s).wait_send()
+        for d in range(2):
+            @pl.when(s < reach - 1)
+            def _():
+                back_copy(d, s).wait_send()
         return carry
 
-    lax.fori_loop(0, chips, finish, 0)
+    lax.fori_loop(0, reach + 1, finish, 0)
 
 
 def local(chips, columns, occupied, occupied_scale, virtual, virtual_scale, trial):
@@ -135,7 +188,10 @@
     any_space = pl.BlockSpec(memory_space=pl.ANY)
     vmem = pl.BlockSpec(memory_space=pltpu.VMEM)
     points = rows * 2 * chips
-    sems = pltpu.SemaphoreType.DMA((3, 2, chips))
+    reach = chips // 2
+    sems = pltpu.SemaphoreType.DMA((3, 2, reach + 1))
+    back_sems = pltpu.SemaphoreType.DMA((2, reach - 1))
+    back_rows = pltpu.VMEM((2, reach - 1, rows // 2, width), jnp.bfloat16)
     return pl.pallas_call(
         functools.partial(kernel, chips, columns),
         out_shape=jax.ShapeDtypeStruct((rows, trial.shape[1]), jnp.float32),
@@ -146,7 +202,10 @@
             pltpu.VMEM((2, 1, width), jnp.float32),
             pltpu.VMEM((rows, width), jnp.bfloat16),
             pltpu.VMEM((rows, width), jnp.bfloat16),
-            sems, sems, sems, sems, pltpu.SemaphoreType.DMA((2,)),
+            pltpu.VMEM((2, reach - 1, 2, rows // 2, width), jnp.bfloat16),
+            pltpu.VMEM((2, reach - 1, rows // 2, width), jnp.float32),
+            back_rows, back_rows,
+            sems, sems, sems, sems, back_sems, back_sems, pltpu.SemaphoreType.DMA((2,)),
         ],
         compiler_params=pltpu.CompilerParams(
             collective_id=0, has_side_effects=True, vmem_limit_bytes=60 * 1024 * 1024),

time: 70.4 us -> 60.2 us (0.86); the launches traced: 69.5 us -> 60 us
  Pallas kernels: 67.6 us -> 58.1 us
    pallas_call x1, Pallas kernels: 67.6 us -> 58.1 us  [local(): pl.pallas_call(functools.partial(kernel, chips, columns), out_shape=jax.S...]
where the time goes in v3:
time: 60.2 us; the launch traced here: 60 us
  Pallas kernels  58.1 us (97%)
  local copies, waits for them, and re-layouts  1.87 us (3%)
    pallas_call x1, Pallas kernels, local(): pl.pallas_call(functools.partial(kernel, chips, columns), out_shape=jax.S...  58.1 us
    unnamed x1, local copies, waits for them, and re-layouts  1.87 us

profile of v3, /device:TPU:0, one launch (start us, length us, event | category | flops | bytes accessed | tf_op | source)
XLA Modules:
  0.0 60.0 jit_solution(16612560684175099600)
XLA Ops:
  0.0 58.1 %shard_map.55 = f32[256,512]{1,0:T(8,128)} custom-call(bf16[256,512]{1,0:T(8,128)(2,1)} %occ_ref.1, f32[1,512]{1,0:T(1,128)} %bitcast.2, bf16[256,512]{1,0:T(8,128)(2,1)} %vir_ref.1, f32[1,512]{1,0:T(1,128)} %bitcast.3, bf16[256,512]{1,0:T(8,128)(2,1)} %tri_ref.1), custom_call_target="tpu_custom_call" | custom-call | flops 3221225472 | bytes 1048576 | tf_op jit(solution)/shard_map/pallas_call | solution.py:195
  58.1 1.9 %copy.7 = f32[256,512]{1,0:T(8,128)} copy(f32[256,512]{1,0:T(8,128)} %shard_map.55) | data formatting | bytes 1048576

commit v4 on v3

--- a/solution.py
+++ b/solution.py
@@ -8,6 +8,7 @@
 from jax.sharding import PartitionSpec as P
 
 MESH = pl.DeviceIdType.MESH
+PIECES = 2
 NT = (((1,), (1,)), ((), ()))
 
 
@@ -25,6 +26,7 @@
     chip = me // 2
     half = buf.shape[-2]
     reach = chips // 2
+    pieces, piece = back.shape[2], back.shape[-1]
     depth = chips // columns
 
     def place_of(q):
@@ -136,35 +138,48 @@
     receive(reach, False)
     receive_twin(reach)
 
-    def back_copy(d, t):
+    def back_copy(d, t, c):
         return pltpu.make_async_remote_copy(
-            src_ref=back.at[d, t], dst_ref=came.at[d, t], send_sem=back_send.at[d, t],
-            recv_sem=back_recv.at[d, t],
+            src_ref=back.at[d, t, c], dst_ref=came.at[d, t, c], send_sem=back_send.at[d, t, c],
+            recv_sem=back_recv.at[d, t, c],
             device_id=(group, before if d == 0 else after), device_id_type=MESH)
 
-    def stage(t, first):
-        e = reach - 1 - t
-        for d in range(2):
-            total = part[d, e - 1] + product(
-                guest[d, e - 1, 0], guest[d, e - 1, 1], 1 - d, slot_of(1 - d, reach))
-            if not first:
-                back_copy(d, t - 1).wait_recv()
-                total += came[d, t - 1].astype(jnp.float32)
-            back[d, t] = total.astype(jnp.bfloat16)
-            back_copy(d, t).start()
-
-    stage(0, True)
+    def columns_of(c):
+        return slice(c * piece, (c + 1) * piece)
+
+    def complete(d, e):
+        return part[d, e - 1] + product(
+            guest[d, e - 1, 0], guest[d, e - 1, 1], 1 - d, slot_of(1 - d, reach))
+
+    for d in range(2):
+        total = complete(d, reach - 1)
+        for c in range(pieces):
+            back[d, 0, c] = total[:, columns_of(c)].astype(jnp.bfloat16)
+            back_copy(d, 0, c).start()
+
+    def complete_later(t, carry):
+        for d in range(2):
+            part[d, reach - 2 - t] = complete(d, reach - 1 - t)
+        return carry
+
+    lax.fori_loop(1, reach - 1, complete_later, 0)
     for d in range(2):
         out_ref[...] += product(so[...], sv[...], d, slot_of(d, reach))
 
     def later_stage(t, carry):
-        stage(t, False)
+        for c in range(pieces):
+            for d in range(2):
+                back_copy(d, t - 1, c).wait_recv()
+                total = part[d, reach - 2 - t, :, columns_of(c)] + came[d, t - 1, c].astype(jnp.float32)
+                back[d, t, c] = total.astype(jnp.bfloat16)
+                back_copy(d, t, c).start()
         return carry
 
     lax.fori_loop(1, reach - 1, later_stage, 0)
-    for d in range(2):
-        back_copy(d, reach - 2).wait_recv()
-        out_ref[pl.ds(d * half, half)] += came[d, reach - 2].astype(jnp.float32)
+    for c in range(pieces):
+        for d in range(2):
+            back_copy(d, reach - 2, c).wait_recv()
+            out_ref[pl.ds(d * half, half), columns_of(c)] += came[d, reach - 2, c].astype(jnp.float32)
 
     def finish(s, carry):
         for a in range(3):
@@ -177,7 +192,8 @@
         for d in range(2):
             @pl.when(s < reach - 1)
             def _():
-                back_copy(d, s).wait_send()
+                for c in range(pieces):
+                    back_copy(d, s, c).wait_send()
         return carry
 
     lax.fori_loop(0, reach + 1, finish, 0)
@@ -190,8 +206,8 @@
     points = rows * 2 * chips
     reach = chips // 2
     sems = pltpu.SemaphoreType.DMA((3, 2, reach + 1))
-    back_sems = pltpu.SemaphoreType.DMA((2, reach - 1))
-    back_rows = pltpu.VMEM((2, reach - 1, rows // 2, width), jnp.bfloat16)
+    back_sems = pltpu.SemaphoreType.DMA((2, reach - 1, PIECES))
+    back_rows = pltpu.VMEM((2, reach - 1, PIECES, rows // 2, width // PIECES), jnp.bfloat16)
     return pl.pallas_call(
         functools.partial(kernel, chips, columns),
         out_shape=jax.ShapeDtypeStruct((rows, trial.shape[1]), jnp.float32),

time: 60.2 us -> 57.6 us (0.957)
  Pallas kernels: 58.1 us -> 55.6 us
    pallas_call x1, Pallas kernels: 58.1 us -> 55.6 us  [local(): pl.pallas_call(functools.partial(kernel, chips, columns), out_shape=jax.S...]
where the time goes in v4:
time: 57.6 us; the launch traced here: 57.5 us
  Pallas kernels  55.6 us (97%)
  local copies, waits for them, and re-layouts  1.87 us (3%)
    pallas_call x1, Pallas kernels, local(): pl.pallas_call(functools.partial(kernel, chips, columns), out_shape=jax.S...  55.6 us
    unnamed x1, local copies, waits for them, and re-layouts  1.87 us

profile of v4, /device:TPU:0, one launch (start us, length us, event | category | flops | bytes accessed | tf_op | source)
XLA Modules:
  0.0 57.5 jit_solution(12249366390925887641)
XLA Ops:
  0.0 55.6 %shard_map.55 = f32[256,512]{1,0:T(8,128)} custom-call(bf16[256,512]{1,0:T(8,128)(2,1)} %occ_ref.1, f32[1,512]{1,0:T(1,128)} %bitcast.2, bf16[256,512]{1,0:T(8,128)(2,1)} %vir_ref.1, f32[1,512]{1,0:T(1,128)} %bitcast.3, bf16[256,512]{1,0:T(8,128)(2,1)} %tri_ref.1), custom_call_target="tpu_custom_call" | custom-call | flops 3221225472 | bytes 1048576 | tf_op jit(solution)/shard_map/pallas_call | solution.py:211
  55.6 1.9 %copy.7 = f32[256,512]{1,0:T(8,128)} copy(f32[256,512]{1,0:T(8,128)} %shard_map.55) | data formatting | bytes 1048576

commit v5 on v4

--- a/solution.py
+++ b/solution.py
@@ -8,7 +8,7 @@
 from jax.sharding import PartitionSpec as P
 
 MESH = pl.DeviceIdType.MESH
-PIECES = 2
+PIECES = 4
 NT = (((1,), (1,)), ((), ()))
 
 
@@ -166,6 +166,18 @@
     for d in range(2):
         out_ref[...] += product(so[...], sv[...], d, slot_of(d, reach))
 
+    def finish(s, carry):
+        for a in range(3):
+            for d in range(2):
+                @pl.when(s < reach)
+                def _():
+                    ring_copy(a, d, s).wait_send()
+
+                pair_copy(a, d, s).wait_send()
+        return carry
+
+    lax.fori_loop(0, reach + 1, finish, 0)
+
     def later_stage(t, carry):
         for c in range(pieces):
             for d in range(2):
@@ -181,22 +193,13 @@
             back_copy(d, reach - 2, c).wait_recv()
             out_ref[pl.ds(d * half, half), columns_of(c)] += came[d, reach - 2, c].astype(jnp.float32)
 
-    def finish(s, carry):
-        for a in range(3):
-            for d in range(2):
-                @pl.when(s < reach)
-                def _():
-                    ring_copy(a, d, s).wait_send()
-
-                pair_copy(a, d, s).wait_send()
-        for d in range(2):
-            @pl.when(s < reach - 1)
-            def _():
-                for c in range(pieces):
-                    back_copy(d, s, c).wait_send()
-        return carry
-
-    lax.fori_loop(0, reach + 1, finish, 0)
+    def finish_back(t, carry):
+        for d in range(2):
+            for c in range(pieces):
+                back_copy(d, t, c).wait_send()
+        return carry
+
+    lax.fori_loop(0, reach - 1, finish_back, 0)
 
 
 def local(chips, columns, occupied, occupied_scale, virtual, virtual_scale, trial):

time: 57.6 us -> 56.6 us (0.983)
  Pallas kernels: 55.6 us -> 54.6 us
    pallas_call x1, Pallas kernels: 55.6 us -> 54.6 us  [local(): pl.pallas_call(functools.partial(kernel, chips, columns), out_shape=jax.S...]
where the time goes in v5:
time: 56.6 us; the launch traced here: 56.5 us
  Pallas kernels  54.6 us (96%)
  local copies, waits for them, and re-layouts  1.87 us (3%)
    pallas_call x1, Pallas kernels, local(): pl.pallas_call(functools.partial(kernel, chips, columns), out_shape=jax.S...  54.6 us
    unnamed x1, local copies, waits for them, and re-layouts  1.87 us

profile of v5, /device:TPU:0, one launch (start us, length us, event | category | flops | bytes accessed | tf_op | source)
XLA Modules:
  0.0 56.5 jit_solution(4741292312800454854)
XLA Ops:
  0.0 54.6 %shard_map.55 = f32[256,512]{1,0:T(8,128)} custom-call(bf16[256,512]{1,0:T(8,128)(2,1)} %occ_ref.1, f32[1,512]{1,0:T(1,128)} %bitcast.2, bf16[256,512]{1,0:T(8,128)(2,1)} %vir_ref.1, f32[1,512]{1,0:T(1,128)} %bitcast.3, bf16[256,512]{1,0:T(8,128)(2,1)} %tri_ref.1), custom_call_target="tpu_custom_call" | custom-call | flops 3221225472 | bytes 1048576 | tf_op jit(solution)/shard_map/pallas_call | solution.py:214
  54.6 1.9 %copy.7 = f32[256,512]{1,0:T(8,128)} copy(f32[256,512]{1,0:T(8,128)} %shard_map.55) | data formatting | bytes 1048576
